TPU v7x, 256 devices: a whole 4x4x8 slice. The times are simulated.
256 devices in a mesh: ctx: 32 (over y, z), tp: 8 (over x, core).
Axes of the slice: x: 4, y: 4, z: 8, core: 2. Of those that a mesh axis runs over, the one named last changes fastest.
Arguments:
- context_block_rows: bfloat16 [16384, 8192], P('ctx', 'tp'), may hold values from -16 to 16
- query_hidden_rows: bfloat16 [64, 8192], P(None, 'tp'), may hold values from -16 to 16
- query_token_positions: int32 [64], replicated, may hold values from 16384 to 16573, as said below
- query_bound: int32 [64], replicated, may hold values from 1 to 16384, as said below
- query_matrix: bfloat16 [8192, 8192], P('ctx', 'tp'), may hold values from -0.0625 to 0.0625
- key_matrix: bfloat16 [8192, 1024], P('ctx', 'tp'), may hold values from -0.0625 to 0.0625
- value_matrix: bfloat16 [8192, 1024], P('ctx', 'tp'), may hold values from -0.0625 to 0.0625
Outputs:
- block_out: bfloat16 [16384, 8192], P('ctx', 'tp')
- query_out: bfloat16 [64, 8192], P(None, 'tp')
Inputs may be any that keep to these rules, and one draw needn't show every extreme that they name: query_token_positions rise strictly with the index; the first is 16384 and the last 16573. `query_bound`: some query token sees all 16384 context tokens.
All inputs are finite; a program needn't handle non-finite values.
Results may differ from a plain program's by a relative error of at most 0.0059.
The roundings to bfloat16 on the way count: a program that leaves them out, or rounds other values in their place, can miss the bound.
Values may be sent and summed in bfloat16 or wider, within the bound.
A program may use at most 128 MiB of HBM per device.

v0:
```python
import math
import jax
import jax.numpy as jnp
from jax import lax
from jax.sharding import PartitionSpec as P

HEAD_SIZE = 128


def from_root(value, axis, source):
    kept = jnp.where(lax.axis_index(axis) == source, value, 0).astype(value.dtype)
    return lax.psum(kept, axis)


def rope_table(half):
    values = []
    for index in range(half):
        freq = 500000.0 ** (-2.0 * index / (2.0 * half))
        wavelen = 2.0 * math.pi / freq
        if wavelen > 8192.0:
            values.append(freq / 8.0)
        elif wavelen < 2048.0:
            values.append(freq)
        else:
            smooth = (8192.0 / wavelen - 1.0) / 3.0
            values.append((1.0 - smooth) * freq / 8.0 + smooth * freq)
    return values


def apply_rotary(values, token_positions):
    half = values.shape[-1] // 2
    freqs = jnp.asarray(rope_table(half), jnp.float32)
    angle = token_positions.astype(jnp.float32)[:, None] * freqs[None, :]
    cosine = jnp.cos(angle)[:, None, :]
    sine = jnp.sin(angle)[:, None, :]
    first = values[..., :half]
    second = values[..., half:]
    return jnp.concatenate([first * cosine - second * sine, second * cosine + first * sine], -1)


def attend(query_heads_split, keys, values, valid):
    scale = 1.0 / math.sqrt(query_heads_split.shape[-1])
    scores = (
        jnp.einsum("qkgd,skd->qkgs", query_heads_split, keys, preferred_element_type=jnp.float32)
        * scale
    )
    scores = jnp.where(valid[:, None, None, :], scores, -1e30)
    peak = jnp.max(scores, -1)
    weights = jnp.exp(scores - peak[..., None])
    total = jnp.sum(weights, -1)
    mixed = jnp.einsum(
        "qkgs,skd->qkgd", weights.astype(jnp.bfloat16), values, preferred_element_type=jnp.float32
    )
    return (peak, total, mixed)


def on_device(
    context_block_rows,
    query_hidden_rows,
    query_token_positions,
    query_bound,
    query_matrix,
    key_matrix,
    value_matrix,
):
    ctx_index = lax.axis_index("ctx")
    blk = context_block_rows.shape[0]
    qcount = query_hidden_rows.shape[0]
    heads_q = query_matrix.shape[1] // HEAD_SIZE
    heads_kv = key_matrix.shape[1] // HEAD_SIZE
    head_group = heads_q // heads_kv
    whole_rows, whole_query = (
        lax.all_gather(context_block_rows, "tp", axis=1, tiled=True),
        lax.all_gather(query_hidden_rows, "tp", axis=1, tiled=True),
    )
    stacked = jnp.concatenate([whole_rows, whole_query], 0)
    head_rows = blk + qcount
    proj_query = jnp.dot(
        stacked,
        lax.all_gather(query_matrix, "ctx", axis=0, tiled=True),
        preferred_element_type=jnp.float32,
    )
    proj_key = jnp.dot(
        stacked,
        lax.all_gather(key_matrix, "ctx", axis=0, tiled=True),
        preferred_element_type=jnp.float32,
    )
    proj_value = jnp.dot(
        stacked,
        lax.all_gather(value_matrix, "ctx", axis=0, tiled=True),
        preferred_element_type=jnp.float32,
    )
    local_pos = ctx_index * blk + jnp.arange(blk, dtype=jnp.int32)
    k_block = apply_rotary(proj_key[:blk].reshape(blk, heads_kv, HEAD_SIZE), local_pos).astype(
        jnp.bfloat16
    )
    v_block = proj_value[:blk].reshape(blk, heads_kv, HEAD_SIZE).astype(jnp.bfloat16)
    key_token_rows = apply_rotary(
        proj_key[blk:head_rows].reshape(qcount, heads_kv, HEAD_SIZE), query_token_positions
    ).astype(jnp.bfloat16)
    value_token_rows = (
        proj_value[blk:head_rows].reshape(qcount, heads_kv, HEAD_SIZE).astype(jnp.bfloat16)
    )
    anchor_key, anchor_value = (from_root(k_block, "ctx", 0), from_root(v_block, "ctx", 0))
    q_block = apply_rotary(proj_query[:blk].reshape(blk, heads_q, HEAD_SIZE), local_pos).astype(
        jnp.bfloat16
    )
    query_token_rows = (
        apply_rotary(proj_query[blk:].reshape(qcount, heads_q, HEAD_SIZE), query_token_positions)
        .astype(jnp.bfloat16)
        .reshape(qcount, heads_kv, head_group, HEAD_SIZE)
    )
    keys_cat = jnp.concatenate([anchor_key, k_block], 0)
    values_cat = jnp.concatenate([anchor_value, v_block], 0)
    anchor_live = ctx_index > 0
    rows_step = min(blk, 512)
    rows_here = 0 + jnp.arange(rows_step, dtype=jnp.int32)
    valid = jnp.concatenate(
        [
            jnp.broadcast_to(anchor_live, (rows_step, blk)),
            rows_here[:, None] >= jnp.arange(blk, dtype=jnp.int32)[None, :],
        ],
        1,
    )
    query_heads_split = q_block.reshape(rows_step, heads_kv, head_group, HEAD_SIZE)
    peak, total, mixed = attend(query_heads_split, keys_cat, values_cat, valid)
    outputs = (
        (mixed / total[..., None]).astype(jnp.bfloat16).reshape(rows_step, heads_q * HEAD_SIZE)
    )
    valid_ctx = local_pos[None, :] < query_bound[:, None]
    peak, total, mixed = attend(query_token_rows, k_block, v_block, valid_ctx)
    top = lax.pmax(peak, "ctx")
    scaled = jnp.exp(peak - top)
    total_all, mixed_all = lax.psum((total * scaled, mixed * scaled[..., None]), "ctx")
    own = jnp.arange(qcount, dtype=jnp.int32)
    self_peak, self_total, self_mixed = attend(
        query_token_rows, key_token_rows, value_token_rows, own[:, None] >= own[None, :]
    )
    final = jnp.maximum(top, self_peak)
    w_ctx = jnp.exp(top - final)
    w_self = jnp.exp(self_peak - final)
    query_out = (mixed_all * w_ctx[..., None] + self_mixed * w_self[..., None]) / (
        total_all * w_ctx + self_total * w_self
    )[..., None]
    query_out = query_out.astype(jnp.bfloat16).reshape(qcount, heads_q * HEAD_SIZE)
    return (outputs, query_out)


def solution(mesh):
    placed = (
        P("ctx", "tp"),
        P(None, "tp"),
        P(),
        P(),
        P("ctx", "tp"),
        P("ctx", "tp"),
        P("ctx", "tp"),
    )
    return jax.shard_map(
        on_device,
        mesh=mesh,
        in_specs=placed,
        out_specs=(P("ctx", "tp"), P(None, "tp")),
        check_vma=False,
    )
```

profile of v0, /device:TPU:2, one launch (start us, length us, event | category | flops | bytes accessed | tf_op | source)
XLA Modules:
  0.0 689.7 jit_solution(3943614140132584248)
XLA Ops:
  11.3 0.9 concatenate.62
  12.3 1.4 broadcast_compare_fusion
  13.6 0.8 multiply_cosine_fusion.3
  14.5 2.5 multiply_cosine_fusion
  17.0 47.3 %all-gather.6.cloned.1.call-done = bf16[512,8192]{1,0:T(8,128)(2,1)} async-done(((bf16[512,1024]{1,0:T(8,128)(2,1)}), bf16[512,8192]{1,0:T(8,128)(2,1)}) %all-gather.6.cloned.1.call-update) | async-done | bytes 8388624 | tf_op jit(solution)/shard_map/all_gather | solution.py:73
  64.3 7.6 %constant_dynamic-update-slice_fusion.1 = bf16[576,8192]{1,0:T(8,128)(2,1)} fusion(bf16[512,8192]{1,0:T(8,128)(2,1)} %all-gather.6.cloned.1.call-done), kind=kLoop, calls=%fused_computation.100 | loop fusion | bytes 16777216
  71.9 19.5 %all-gather.8.cloned.1.call-done = bf16[64,8192]{1,0:T(8,128)(2,1)} async-done(((bf16[64,1024]{1,0:T(8,128)(2,1)}), bf16[64,8192]{1,0:T(8,128)(2,1)}) %all-gather.8.cloned.1.call-update) | async-done | bytes 1048592 | tf_op jit(solution)/shard_map/all_gather | solution.py:74
  91.4 2.3 constant_dynamic-update-slice_fusion
  93.7 79.8 %all-gather.12.cloned.1.call-done = bf16[8192,128]{1,0:T(8,128)(2,1)} async-done(((bf16[256,128]{1,0:T(8,128)(2,1)}), bf16[8192,128]{1,0:T(8,128)(2,1)}) %all-gather.12.cloned.1.call-update) | async-done | bytes 2097168 | tf_op jit(solution)/shard_map/all_gather | solution.py:85
  173.5 5.8 fusion.83
  179.4 1.2 fusion.35
  180.6 0.8 maximum_select_fusion
  181.4 0.8 fusion.64
  182.2 68.9 %all-gather.10.cloned.1.call-done = bf16[8192,128]{1,0:T(8,128)(2,1)} async-done(((bf16[256,128]{1,0:T(8,128)(2,1)}), bf16[8192,128]{1,0:T(8,128)(2,1)}) %all-gather.10.cloned.1.call-update) | async-done | bytes 2097168 | tf_op jit(solution)/shard_map/all_gather | solution.py:90
  251.1 6.9 convolution_convert_fusion
  258.0 0.7 slice_bitcast_fusion.3
  258.9 132.5 %all-gather.14.cloned.1.call-done = bf16[8192,1024]{1,0:T(8,128)(2,1)} async-done(((bf16[256,1024]{1,0:T(8,128)(2,1)}), bf16[8192,1024]{1,0:T(8,128)(2,1)}) %all-gather.14.cloned.1.call-update) | async-done | bytes 16777232 | tf_op jit(solution)/shard_map/all_gather | solution.py:80
  391.4 14.9 %fusion.84 = f32[576,1024]{1,0:T(8,128)S(1)} fusion(bf16[576,8192]{1,0:T(8,128)(2,1)} %constant_dynamic-update-slice_fusion, bf16[8192,1024]{1,0:T(8,128)(2,1)} %all-gather.14.cloned.1.call-done), kind=kOutput, calls=%fused_computation.126 | convolution fusion | flops 9663676416 | bytes 28573696 | tf_op jit(solution)/shard_map/dot_general | solution.py:78
  406.8 1.4 fusion.81
  408.2 1.0 fusion.25
  409.1 71.4 %pmax.7 = f32[64,1,8]{0,2,1:T(8,128)S(1)} all-reduce(f32[64,1,8]{0,2,1:T(8,128)S(1)} %bitcast.169), channel_id=1, replica_groups=mesh['ctx'=32,'tp'=8] {'ctx'}, use_global_device_ids=true, to_apply=%region_5.6 | all-reduce | flops 512 | bytes 4096 | tf_op jit(solution)/shard_map/pmax | solution.py:132
  481.1 2.0 fusion.79
  483.7 1.1 fusion.14
  484.8 3.5 subtract_convert_fusion
  488.2 47.8 %all-reduce.7.cloned.1.call-done = (bf16[512,1,128]{2,0,1:T(8,128)(2,1)}, bf16[512,1,128]{2,0,1:T(8,128)(2,1)}) async-done(((bf16[512,1,128]{2,0,1:T(8,128)(2,1)}, bf16[512,1,128]{2,0,1:T(8,128)(2,1)}), (bf16[512,1,128]{2,0,1:T(8,128)(2,1)}, bf16[512,1,128]{2,0,1:T(8,128)(2,1)})) %all-reduce.7.cloned.1.call-update) | async-done | bytes 262160 | tf_op jit(solution)/shard_map/psum | solution.py:12
  536.1 10.7 %fusion.2 = (f32[512,8]{0,1:T(8,128)S(1)}, f32[1024,512,8]{1,0,2:T(8,128)}) fusion(pred[512,1024]{0,1:T(8,128)(4,1)} %concatenate.62, bf16[512,8,64]{2,0,1:T(8,128)(2,1)} %get-tuple-element.9, bf16[512,8,64]{2,0,1:T(8,128)(2,1)S(1)} %get-tuple-element.8, bf16[512,1,64]{2,0,1:T(8,128)(2,1)} %copy-done.1, bf16[512,1,64]{2,0,1:T(8,128)(2,1)S(1)} %get-tuple-element.14, ...), kind=kOutput, calls=%fused_computation.4 | convolution fusion | flops 1089204224 | bytes 18628608 | tf_op jit(solution)/shard_map/qkgd,skd->qkgs/dot_general | solution.py:44
  546.8 9.3 %fusion = f32[512,8]{0,1:T(8,128)S(1)} fusion(f32[1024,512,8]{1,0,2:T(8,128)} %get-tuple-element.32, f32[512,8]{0,1:T(8,128)S(1)} %get-tuple-element.31, pred[512,1024]{0,1:T(8,128)(4,1)S(1)} %copy-done), kind=kLoop, calls=%fused_computation.2 | loop fusion | flops 16773120 | bytes 17334272 | tf_op jit(solution)/shard_map/reduce_sum | solution.py:50
  556.5 9.1 %fusion.7 = bf16[1,128,512,8]{2,1,3,0:T(8,128)(2,1)S(1)} fusion(f32[1024,512,8]{1,0,2:T(8,128)} %get-tuple-element.32, f32[512,8]{0,1:T(8,128)S(1)} %get-tuple-element.31, pred[512,1024]{0,1:T(8,128)(4,1)S(1)} %copy-done, f32[512,8]{0,1:T(8,128)S(1)} %fusion, bf16[512,1,128]{2,0,1:T(8,128)(2,1)S(1)} %copy-done.4, bf16[512,1,128]{2,0,1:T(8,128)(2,1)S(1)} %copy-done.10), kind=kOutput, calls=%fused_computation.10 | convolution fusion | flops 1092091904 | bytes 18644992 | tf_op jit(solution)/shard_map/qkgs,skd->qkgd/dot_general | solution.py:51
  565.7 1.3 copy.29
  567.0 72.5 %psum.31 = f32[64,1,8]{0,2,1:T(8,128)S(1)} all-reduce(f32[64,1,8]{0,2,1:T(8,128)S(1)} %copy-done.8), channel_id=1, replica_groups=mesh['ctx'=32,'tp'=8] {'ctx'}, use_global_device_ids=true, to_apply=%region_9.10 | all-reduce | flops 512 | bytes 4096 | tf_op jit(solution)/shard_map/psum | solution.py:134
  639.5 41.2 %all-reduce.5.cloned.1.call-done = f32[64,1,8,128]{3,0,2,1:T(8,128)} async-done(((f32[64,1,8,128]{3,0,2,1:T(8,128)}), f32[64,1,8,128]{3,0,2,1:T(8,128)}) %all-reduce.5.cloned.1.call-update) | async-done | bytes 262160 | tf_op jit(solution)/shard_map/psum | solution.py:134
  680.7 1.3 fusion.19
  (55 shorter events, 6.9 us)
Async XLA Ops:
  7.2 57.1 %all-gather.6.cloned.1.call-start = ((), (), s32[]{:S(2)}) async-start(), calls=%async_computation | async-start | bytes 9437184 | tf_op jit(solution)/shard_map/all_gather | solution.py:73
  7.9 83.5 %all-gather.8.cloned.1.call-start = ((), (), s32[]{:S(2)}) async-start(), calls=%async_computation.1 | async-start | bytes 1179648 | tf_op jit(solution)/shard_map/all_gather | solution.py:74
  8.6 164.9 %all-gather.12.cloned.1.call-start = ((), (), s32[]{:S(2)}) async-start(), calls=%async_computation.3 | async-start | bytes 2162688 | tf_op jit(solution)/shard_map/all_gather | solution.py:85
  9.4 241.7 %all-gather.10.cloned.1.call-start = ((), (), s32[]{:S(2)}) async-start(), calls=%async_computation.2 | async-start | bytes 2162688 | tf_op jit(solution)/shard_map/all_gather | solution.py:90
  10.0 381.4 %all-gather.14.cloned.1.call-start = ((), (), s32[]{:S(2)}) async-start(), calls=%async_computation.4 | async-start | bytes 17301504 | tf_op jit(solution)/shard_map/all_gather | solution.py:80
  10.5 525.5 %all-reduce.7.cloned.1.call-start = ((), (), s32[]{:S(2)}) async-start(), calls=%async_computation.6 | async-start | bytes 524288 | tf_op jit(solution)/shard_map/psum | solution.py:12
  71.9 107.5 %copy-start.9 = (f32[64]{0:T(128)S(1)}, f32[64]{0:T(128)}, u32[]{:S(2)}) copy-start(f32[64]{0:T(128)} %constant.24.clone) | copy-start | bytes 772
  180.6 225.7 %copy-start.1 = (bf16[512,1,64]{2,0,1:T(8,128)(2,1)}, bf16[512,1,64]{2,0,1:T(8,128)(2,1)S(1)}, u32[]{:S(2)}) copy-start(bf16[512,1,64]{2,0,1:T(8,128)(2,1)S(1)} %get-tuple-element.15) | copy-start | bytes 196612
  258.0 133.4 %copy-start.2 = (bf16[576,128]{1,0:T(8,128)(2,1)}, bf16[576,128]{1,0:T(8,128)(2,1)S(1)}, u32[]{:S(2)}) copy-start(bf16[576,128]{1,0:T(8,128)(2,1)S(1)} %convolution_convert_fusion) | copy-start | bytes 442372
  258.8 421.9 %all-reduce.5.cloned.1.call-start = ((), (), s32[]{:S(2)}) async-start(), calls=%async_computation.5 | async-start | bytes 524288 | tf_op jit(solution)/shard_map/psum | solution.py:134
  480.6 2.5 copy-start.7
  480.6 3.1 copy-start.3
  536.1 10.7 %copy-start = (pred[512,1024]{0,1:T(8,128)(4,1)S(1)}, pred[512,1024]{0,1:T(8,128)(4,1)}, u32[]{:S(2)}) copy-start(pred[512,1024]{0,1:T(8,128)(4,1)} %concatenate.62) | copy-start | bytes 1572868
  546.8 9.3 %copy-start.5 = (bf16[64,64]{1,0:T(8,128)(2,1)S(1)}, bf16[64,64]{1,0:T(8,128)(2,1)}, u32[]{:S(2)}) copy-start(bf16[64,64]{1,0:T(8,128)(2,1)} %get-tuple-element.20) | copy-start | bytes 24580
  546.8 9.3 %copy-start.6 = (bf16[64,64]{1,0:T(8,128)(2,1)S(1)}, bf16[64,64]{1,0:T(8,128)(2,1)}, u32[]{:S(2)}) copy-start(bf16[64,64]{1,0:T(8,128)(2,1)} %get-tuple-element.21) | copy-start | bytes 24580
  546.8 9.6 %copy-start.4 = (bf16[512,1,128]{2,0,1:T(8,128)(2,1)S(1)}, bf16[512,1,128]{2,0,1:T(8,128)(2,1)}, u32[]{:S(2)}) copy-start(bf16[512,1,128]{2,0,1:T(8,128)(2,1)} %get-tuple-element.18) | copy-start | bytes 393220
  546.8 9.6 %copy-start.10 = (bf16[512,1,128]{2,0,1:T(8,128)(2,1)S(1)}, bf16[512,1,128]{2,0,1:T(8,128)(2,1)}, u32[]{:S(2)}) copy-start(bf16[512,1,128]{2,0,1:T(8,128)(2,1)} %get-tuple-element.7) | copy-start | bytes 393220
  556.5 10.5 %copy-start.8 = (f32[64,1,8]{0,2,1:T(8,128)S(1)}, f32[64,1,8]{0,2,1:T(8,128)}, u32[]{:S(2)}) copy-start(f32[64,1,8]{0,2,1:T(8,128)} %get-tuple-element.25) | copy-start | bytes 6148
Sparse Core Ops, SparseCore 0:
  9.8 54.4 all-gather.5
  66.1 25.2 all-gather.7
  94.0 79.4 all-gather.11
  176.0 75.1 all-gather.9
  253.6 137.7 all-gather.13
  394.7 141.2 all-reduce.6
  539.5 141.1 all-reduce.4
where the time goes:
time: 690 us
  waiting for transfers between devices  440 us (64%)
  blocking collectives  144 us (21%)
  matrix products  51.5 us (7%)
  other arithmetic  23.5 us (3%)
  local copies, waits for them, and re-layouts  15.8 us (2%)
  between operations  14.4 us (2%)
    all_gather x1, waiting for transfers between devices, on_device(): lax.all_gather(query_matrix, 'ctx', axis=0, tiled=True)  133 us
    all_gather x1, waiting for transfers between devices, on_device(): lax.all_gather(key_matrix, 'ctx', axis=0, tiled=True)  79.8 us
    psum x1, blocking collectives, on_device(): lax.psum((total * scaled, mixed * scaled[..., None]), 'ctx')  72.5 us
    pmax x1, blocking collectives, on_device(): top = lax.pmax(peak, 'ctx')  71.4 us
    all_gather x1, waiting for transfers between devices, on_device(): lax.all_gather(value_matrix, 'ctx', axis=0, tiled=True)  68.9 us
    psum x1, waiting for transfers between devices, from_root(): return lax.psum(kept, axis)  47.8 us
    all_gather x1, waiting for transfers between devices, on_device(): lax.all_gather(context_block_rows, 'tp', axis=1, tiled=True)  47.3 us
    psum x1, waiting for transfers between devices, on_device(): lax.psum((total * scaled, mixed * scaled[..., None]), 'ctx')  41.2 us
  transfers between devices with their start and end apart: 7, of which 7 were waited for; matrix products, arithmetic and copies ran while one was open for 13% of the time, Pallas kernels for 0%

commit v1 on v0

--- a/solution.py
+++ b/solution.py
@@ -5,6 +5,9 @@
 from jax.sharding import PartitionSpec as P
 
 HEAD_SIZE = 128
+series_all_clear = lambda w_in, array_dim: jnp.concatenate(
+    lax.all_to_all(jnp.stack([w_in for _ in range(lax.psum(1, "tp"))]), "tp", 0, 0), axis=array_dim
+)
 
 
 def from_root(value, axis, source):
@@ -70,7 +73,7 @@
     heads_kv = key_matrix.shape[1] // HEAD_SIZE
     head_group = heads_q // heads_kv
     whole_rows, whole_query = (
-        lax.all_gather(context_block_rows, "tp", axis=1, tiled=True),
+        series_all_clear(context_block_rows, 1),
         lax.all_gather(query_hidden_rows, "tp", axis=1, tiled=True),
     )
     stacked = jnp.concatenate([whole_rows, whole_query], 0)

time: 690 us -> 652 us (0.945)
  waiting for transfers between devices: 440 us -> 398 us
  starting transfers between devices: 0.27 us -> 7.66 us
    all_gather x1 -> x0, waiting for transfers between devices: 47.3 us -> none  [on_device(): lax.all_gather(context_block_rows, 'tp', axis=1, tiled=True)]
    all_gather x1, waiting for transfers between devices: 19.5 us -> 27.5 us  [on_device(): lax.all_gather(query_hidden_rows, 'tp', axis=1, tiled=True)]
    all_to_all x0 -> x1, starting transfers between devices: none -> 7.28 us  [lax.all_to_all(jnp.stack([w_in for _ in range(lax.psum(1, 'tp'))]), 'tp',...]
  transfers between devices with their start and end apart: 7 -> 7, of which waited for: 7 -> 6; matrix products, arithmetic and copies ran while one was open for 13% -> 13% of each run, Pallas kernels for 0% -> 0%
where the time goes in v1:
time: 652 us
  waiting for transfers between devices  398 us (61%)
  blocking collectives  144 us (22%)
  matrix products  54.5 us (8%)
  other arithmetic  20.8 us (3%)
  between operations  14.4 us (2%)
  local copies, waits for them, and re-layouts  13.2 us (2%)
  starting transfers between devices  7.66 us (1%)
    all_gather x1, waiting for transfers between devices, on_device(): lax.all_gather(query_matrix, 'ctx', axis=0, tiled=True)  132 us
    all_gather x1, waiting for transfers between devices, on_device(): lax.all_gather(key_matrix, 'ctx', axis=0, tiled=True)  80.8 us
    psum x1, blocking collectives, on_device(): lax.psum((total * scaled, mixed * scaled[..., None]), 'ctx')  72.5 us
    pmax x1, blocking collectives, on_device(): top = lax.pmax(peak, 'ctx')  71.3 us
    all_gather x1, waiting for transfers between devices, on_device(): lax.all_gather(value_matrix, 'ctx', axis=0, tiled=True)  67.3 us
    psum x1, waiting for transfers between devices, from_root(): return lax.psum(kept, axis)  46.9 us
    psum x1, waiting for transfers between devices, on_device(): lax.psum((total * scaled, mixed * scaled[..., None]), 'ctx')  41.1 us
    all_gather x1, waiting for transfers between devices, on_device(): lax.all_gather(query_hidden_rows, 'tp', axis=1, tiled=True)  27.5 us
  transfers between devices with their start and end apart: 7, of which 6 were waited for; matrix products, arithmetic and copies ran while one was open for 13% of the time, Pallas kernels for 0%

profile of v1, /device:TPU:2, one launch (start us, length us, event | category | flops | bytes accessed | tf_op | source)
XLA Modules:
  0.0 652.1 jit_solution(15494533580177052752)
XLA Ops:
  7.2 1.7 copy.22
  9.0 0.7 all-gather.9.cloned.1.call-update
  11.0 1.5 copy.21
  12.5 4.0 stack.2
  16.5 7.3 %all-to-all-start = ((bf16[8,512,1024]{1,2,0:T(8,128)(2,1)}), bf16[8,512,1024]{1,2,0:T(8,128)(2,1)}, u32[]{:S(2)}, u32[]{:S(2)}) async-start(bf16[8,512,1024]{1,2,0:T(8,128)(2,1)} %stack.2), calls=%async_computation | async-start | bytes 16777216 | tf_op jit(solution)/shard_map/all_to_all | solution.py:9
  23.9 0.9 concatenate.62
  25.7 1.8 multiply_cosine_fusion
  27.6 27.5 %all-gather.5.cloned.1.call-done = bf16[64,8192]{0,1:T(8,128)(2,1)} async-done(((bf16[64,1024]{0,1:T(8,128)(2,1)}), bf16[64,8192]{0,1:T(8,128)(2,1)}) %all-gather.5.cloned.1.call-update) | async-done | bytes 1048592 | tf_op jit(solution)/shard_map/all_gather | solution.py:77
  55.1 80.8 %all-gather.9.cloned.1.call-done = bf16[8192,128]{1,0:T(8,128)(2,1)} async-done(((bf16[256,128]{1,0:T(8,128)(2,1)}), bf16[8192,128]{1,0:T(8,128)(2,1)}) %all-gather.9.cloned.1.call-update) | async-done | bytes 2097168 | tf_op jit(solution)/shard_map/all_gather | solution.py:88
  135.9 7.6 %fusion.8 = f32[576,128]{1,0:T(8,128)S(1)} fusion(bf16[8192,128]{1,0:T(8,128)(2,1)} %all-gather.9.cloned.1.call-done, bf16[64,8192]{0,1:T(8,128)(2,1)} %all-gather.5.cloned.1.call-done, bf16[512,8192]{0,1:T(8,128)(2,1)} %bitcast.1), kind=kOutput, calls=%fused_computation.10 | convolution fusion | flops 1226833920 | bytes 11829248 | tf_op jit(solution)/shard_map/dot_general | solution.py:86
  143.6 1.2 fusion.39
  144.8 0.8 maximum_select_fusion
  145.6 0.8 fusion.68
  146.4 67.3 %all-gather.7.cloned.1.call-done = bf16[8192,128]{1,0:T(8,128)(2,1)} async-done(((bf16[256,128]{1,0:T(8,128)(2,1)}), bf16[8192,128]{1,0:T(8,128)(2,1)}) %all-gather.7.cloned.1.call-update) | async-done | bytes 2097168 | tf_op jit(solution)/shard_map/all_gather | solution.py:93
  213.7 7.1 %fusion.22 = bf16[576,128]{1,0:T(8,128)(2,1)S(1)} fusion(bf16[8192,128]{1,0:T(8,128)(2,1)} %all-gather.7.cloned.1.call-done, bf16[64,8192]{0,1:T(8,128)(2,1)S(1)} %copy-done.11, bf16[512,8192]{0,1:T(8,128)(2,1)} %bitcast.1), kind=kOutput, calls=%fused_computation.30 | convolution fusion | flops 1226907648 | bytes 11681792 | tf_op jit(solution)/shard_map/dot_general | solution.py:91
  220.8 0.7 slice_bitcast_fusion.3
  221.8 132.2 %all-gather.11.cloned.1.call-done = bf16[8192,1024]{1,0:T(8,128)(2,1)} async-done(((bf16[256,1024]{1,0:T(8,128)(2,1)}), bf16[8192,1024]{1,0:T(8,128)(2,1)}) %all-gather.11.cloned.1.call-update) | async-done | bytes 16777232 | tf_op jit(solution)/shard_map/all_gather | solution.py:83
  354.0 15.9 %fusion.7 = f32[576,1024]{1,0:T(8,128)S(1)} fusion(bf16[8192,1024]{1,0:T(8,128)(2,1)} %all-gather.11.cloned.1.call-done, bf16[64,8192]{0,1:T(8,128)(2,1)S(1)} %copy-done.11, bf16[512,8192]{0,1:T(8,128)(2,1)} %bitcast.1), kind=kOutput, calls=%fused_computation.9 | convolution fusion | flops 9682550784 | bytes 28573696 | tf_op jit(solution)/shard_map/dot_general | solution.py:81
  370.5 1.4 fusion.88
  371.9 1.0 fusion.29
  372.8 71.3 %pmax.7 = f32[64,1,8]{0,2,1:T(8,128)S(1)} all-reduce(f32[64,1,8]{0,2,1:T(8,128)S(1)} %bitcast.169), channel_id=1, replica_groups=mesh['ctx'=32,'tp'=8] {'ctx'}, use_global_device_ids=true, to_apply=%region_5.6 | all-reduce | flops 512 | bytes 4096 | tf_op jit(solution)/shard_map/pmax | solution.py:135
  444.6 2.0 fusion.86
  447.2 1.1 fusion.17
  448.3 3.5 subtract_convert_fusion
  451.8 46.9 %all-reduce.7.cloned.1.call-done = (bf16[512,1,128]{2,0,1:T(8,128)(2,1)}, bf16[512,1,128]{2,0,1:T(8,128)(2,1)}) async-done(((bf16[512,1,128]{2,0,1:T(8,128)(2,1)}, bf16[512,1,128]{2,0,1:T(8,128)(2,1)}), (bf16[512,1,128]{2,0,1:T(8,128)(2,1)}, bf16[512,1,128]{2,0,1:T(8,128)(2,1)})) %all-reduce.7.cloned.1.call-update) | async-done | bytes 262160 | tf_op jit(solution)/shard_map/psum | solution.py:15
  498.6 10.7 %fusion.2 = (f32[512,8]{0,1:T(8,128)S(1)}, f32[1024,512,8]{1,0,2:T(8,128)}) fusion(pred[512,1024]{0,1:T(8,128)(4,1)} %concatenate.62, bf16[512,8,64]{2,0,1:T(8,128)(2,1)} %get-tuple-element.9, bf16[512,8,64]{2,0,1:T(8,128)(2,1)S(1)} %get-tuple-element.8, bf16[512,1,64]{2,0,1:T(8,128)(2,1)} %copy-done.1, bf16[512,1,64]{2,0,1:T(8,128)(2,1)S(1)} %get-tuple-element.14, ...), kind=kOutput, calls=%fused_computation.4 | convolution fusion | flops 1089204224 | bytes 18628608 | tf_op jit(solution)/shard_map/qkgd,skd->qkgs/dot_general | solution.py:47
  509.4 9.3 %fusion = f32[512,8]{0,1:T(8,128)S(1)} fusion(f32[1024,512,8]{1,0,2:T(8,128)} %get-tuple-element.32, f32[512,8]{0,1:T(8,128)S(1)} %get-tuple-element.31, pred[512,1024]{0,1:T(8,128)(4,1)S(1)} %copy-done), kind=kLoop, calls=%fused_computation.2 | loop fusion | flops 16773120 | bytes 17334272 | tf_op jit(solution)/shard_map/reduce_sum | solution.py:53
  519.0 9.1 %fusion.10 = bf16[1,128,512,8]{2,1,3,0:T(8,128)(2,1)S(1)} fusion(f32[1024,512,8]{1,0,2:T(8,128)} %get-tuple-element.32, f32[512,8]{0,1:T(8,128)S(1)} %get-tuple-element.31, pred[512,1024]{0,1:T(8,128)(4,1)S(1)} %copy-done, f32[512,8]{0,1:T(8,128)S(1)} %fusion, bf16[512,1,128]{2,0,1:T(8,128)(2,1)S(1)} %copy-done.4, bf16[512,1,128]{2,0,1:T(8,128)(2,1)S(1)} %copy-done.12), kind=kOutput, calls=%fused_computation.14 | convolution fusion | flops 1092091904 | bytes 18644992 | tf_op jit(solution)/shard_map/qkgs,skd->qkgd/dot_general | solution.py:54
  528.2 1.3 copy.31
  529.5 72.5 %psum.31 = f32[64,1,8]{0,2,1:T(8,128)S(1)} all-reduce(f32[64,1,8]{0,2,1:T(8,128)S(1)} %copy-done.8), channel_id=1, replica_groups=mesh['ctx'=32,'tp'=8] {'ctx'}, use_global_device_ids=true, to_apply=%region_9.10 | all-reduce | flops 512 | bytes 4096 | tf_op jit(solution)/shard_map/psum | solution.py:137
  602.1 41.1 %all-reduce.5.cloned.1.call-done = f32[64,1,8,128]{3,0,2,1:T(8,128)} async-done(((f32[64,1,8,128]{3,0,2,1:T(8,128)}), f32[64,1,8,128]{3,0,2,1:T(8,128)}) %all-reduce.5.cloned.1.call-update) | async-done | bytes 262160 | tf_op jit(solution)/shard_map/psum | solution.py:137
  643.2 1.3 fusion.23
  (61 shorter events, 5.5 us)
Async XLA Ops:
  7.2 47.9 %all-gather.5.cloned.1.call-start = ((), (), s32[]{:S(2)}) async-start(), calls=%async_computation.1 | async-start | bytes 2359296 | tf_op jit(solution)/shard_map/all_gather | solution.py:77
  9.0 126.9 %all-gather.9.cloned.1.call-start = ((), (), s32[]{:S(2)}) async-start(), calls=%async_computation.3 | async-start | bytes 2162688 | tf_op jit(solution)/shard_map/all_gather | solution.py:88
  9.7 204.0 %all-gather.7.cloned.1.call-start = ((), (), s32[]{:S(2)}) async-start(), calls=%async_computation.2 | async-start | bytes 2162688 | tf_op jit(solution)/shard_map/all_gather | solution.py:93
  10.5 343.5 %all-gather.11.cloned.1.call-start = ((), (), s32[]{:S(2)}) async-start(), calls=%async_computation.4 | async-start | bytes 17301504 | tf_op jit(solution)/shard_map/all_gather | solution.py:83
  16.5 7.3 %copy-start.13 = (s32[64]{0:T(128)S(1)}, s32[64]{0:T(128)}, u32[]{:S(2)}) copy-start(s32[64]{0:T(128)} %param.13) | copy-start | bytes 772
  16.5 8.3 %copy-start.10 = (s32[64]{0:T(128)S(1)}, s32[64]{0:T(128)}, u32[]{:S(2)}) copy-start(s32[64]{0:T(128)} %param.14) | copy-start | bytes 772
  16.5 9.0 %copy-start.9 = (f32[64]{0:T(128)S(1)}, f32[64]{0:T(128)}, u32[]{:S(2)}) copy-start(f32[64]{0:T(128)} %constant.24.clone) | copy-start | bytes 772
  16.5 119.4 %all-to-all-start = ((bf16[8,512,1024]{1,2,0:T(8,128)(2,1)}), bf16[8,512,1024]{1,2,0:T(8,128)(2,1)}, u32[]{:S(2)}, u32[]{:S(2)}) async-start(bf16[8,512,1024]{1,2,0:T(8,128)(2,1)} %stack.2), calls=%async_computation | async-start | bytes 16777216 | tf_op jit(solution)/shard_map/all_to_all | solution.py:9
  23.8 474.9 %all-reduce.7.cloned.1.call-start = ((), (), s32[]{:S(2)}) async-start(), calls=%async_computation.6 | async-start | bytes 524288 | tf_op jit(solution)/shard_map/psum | solution.py:15
  135.9 77.8 %copy-start.11 = (bf16[64,8192]{0,1:T(8,128)(2,1)S(1)}, bf16[64,8192]{0,1:T(8,128)(2,1)}, u32[]{:S(2)}) copy-start(bf16[64,8192]{0,1:T(8,128)(2,1)} %all-gather.5.cloned.1.call-done) | copy-start | bytes 3145732
  144.8 76.0 %copy-start.1 = (bf16[512,1,64]{2,0,1:T(8,128)(2,1)}, bf16[512,1,64]{2,0,1:T(8,128)(2,1)S(1)}, u32[]{:S(2)}) copy-start(bf16[512,1,64]{2,0,1:T(8,128)(2,1)S(1)} %get-tuple-element.15) | copy-start | bytes 196612
  220.8 133.2 %copy-start.2 = (bf16[576,128]{1,0:T(8,128)(2,1)}, bf16[576,128]{1,0:T(8,128)(2,1)S(1)}, u32[]{:S(2)}) copy-start(bf16[576,128]{1,0:T(8,128)(2,1)S(1)} %fusion.22) | copy-start | bytes 442372
  221.5 421.6 %all-reduce.5.cloned.1.call-start = ((), (), s32[]{:S(2)}) async-start(), calls=%async_computation.5 | async-start | bytes 524288 | tf_op jit(solution)/shard_map/psum | solution.py:137
  444.1 2.5 copy-start.7
  444.1 3.1 copy-start.3
  498.6 10.7 %copy-start = (pred[512,1024]{0,1:T(8,128)(4,1)S(1)}, pred[512,1024]{0,1:T(8,128)(4,1)}, u32[]{:S(2)}) copy-start(pred[512,1024]{0,1:T(8,128)(4,1)} %concatenate.62) | copy-start | bytes 1572868
  509.3 9.3 %copy-start.5 = (bf16[64,64]{1,0:T(8,128)(2,1)S(1)}, bf16[64,64]{1,0:T(8,128)(2,1)}, u32[]{:S(2)}) copy-start(bf16[64,64]{1,0:T(8,128)(2,1)} %get-tuple-element.20) | copy-start | bytes 24580
  509.3 9.3 %copy-start.6 = (bf16[64,64]{1,0:T(8,128)(2,1)S(1)}, bf16[64,64]{1,0:T(8,128)(2,1)}, u32[]{:S(2)}) copy-start(bf16[64,64]{1,0:T(8,128)(2,1)} %get-tuple-element.21) | copy-start | bytes 24580
  509.3 9.6 %copy-start.4 = (bf16[512,1,128]{2,0,1:T(8,128)(2,1)S(1)}, bf16[512,1,128]{2,0,1:T(8,128)(2,1)}, u32[]{:S(2)}) copy-start(bf16[512,1,128]{2,0,1:T(8,128)(2,1)} %get-tuple-element.18) | copy-start | bytes 393220
  509.4 9.6 %copy-start.12 = (bf16[512,1,128]{2,0,1:T(8,128)(2,1)S(1)}, bf16[512,1,128]{2,0,1:T(8,128)(2,1)}, u32[]{:S(2)}) copy-start(bf16[512,1,128]{2,0,1:T(8,128)(2,1)} %get-tuple-element.7) | copy-start | bytes 393220
  519.0 10.5 %copy-start.8 = (f32[64,1,8]{0,2,1:T(8,128)S(1)}, f32[64,1,8]{0,2,1:T(8,128)}, u32[]{:S(2)}) copy-start(f32[64,1,8]{0,2,1:T(8,128)} %get-tuple-element.25) | copy-start | bytes 6148
Sparse Core Ops, SparseCore 0:
  10.4 44.5 all-gather.4
  57.7 78.2 all-gather.8
  138.5 75.1 all-gather.6
  216.1 137.7 all-gather.10
  357.3 141.2 all-reduce.6
  502.0 141.1 all-reduce.4
